TPU v7x, 128 devices: a whole 4x4x4 slice. The times are simulated.
128 devices in a mesh: section: 8 (over x_hi, y), ctx: 16 (over z, x_lo, core).
Axes of the slice: x: 4 (x_hi: 2, x_lo: 2; x = x_hi * 2 + x_lo), y: 4, z: 4, core: 2. Of those that a mesh axis runs over, the one named last changes fastest.
Arguments:
- down_in: bfloat16 [8, 2048, 4096], P('section', 'ctx')
- up_in: bfloat16 [8, 2048, 4096], P('section', 'ctx')
- down_cot: bfloat16 [8, 2048, 4096], P('section', 'ctx'), may hold values from -6 to 6
- up_cot: bfloat16 [8, 2048, 4096], P('section', 'ctx'), may hold values from -6 to 6
- kv_weight: bfloat16 [2, 8, 4096, 1024], P(None, 'section'), as said below
- norm_gain: float32 [2, 8, 4096], P(None, 'section'), as said below
- span_ids: int32 [16], replicated, may hold values from 0 to 15, each once
Outputs:
- down_out: bfloat16 [8, 2048, 4096], P('section', 'ctx')
- up_out: bfloat16 [8, 2048, 4096], P('section', 'ctx')
- down_grad: bfloat16 [8, 2048, 4096], P('section', 'ctx')
- up_grad: bfloat16 [8, 2048, 4096], P('section', 'ctx')
- kv_grad: float32 [8, 4096, 1024], P('section', 'ctx')
- gain_grad: float32 [8, 4096], P('section', 'ctx')
Inputs may be any that keep to these rules, and one draw needn't show every extreme that they name: kv_weight[1, s] equals kv_weight[0, 7 - s]: copy 1 is the layer of the mirrored section. norm_gain[1, s] equals norm_gain[0, 7 - s]; all entries are positive.
All inputs are finite; a program needn't handle non-finite values.
Results may differ from a plain program's by a relative error of at most 0.027.
Values may be sent and summed in bfloat16 or wider, within the bound.
A program may use at most 192 MiB of HBM per device.

v0:
```python
import functools

import jax
import jax.numpy as jnp
from jax import lax
from jax.experimental import pallas as pl
from jax.experimental.pallas import tpu as pltpu
from jax.sharding import PartitionSpec as P

LOG2E = 1.4426950408889634
NT = (((1,), (1,)), ((), ()))
TN = (((0,), (0,)), ((), ()))
F32 = jnp.float32
BF = jnp.bfloat16


def stack_heads(block):
    return jnp.concatenate([block[:, j * 128:(j + 1) * 128] for j in range(8)], 0)


def spread_heads(rows):
    return jnp.concatenate([rows[j * 128:(j + 1) * 128] for j in range(8)], 1)


def attention_kernel(block, small, tq_ref, inv_ref, q_own, q_got, dy_own, dy_got, x_own, x_got, kv_hbm,
                     y_own, y_got, dq_own, dq_got, terms_ref, kv_s, dk_s, dv_s, e_s, top_s, sems):
    head = pl.program_id(0)
    spans = kv_hbm.shape[0]
    heads = kv_hbm.shape[2] // 256
    scale = 128 ** -0.5
    c = scale * LOG2E

    def load(h, t):
        return pltpu.make_async_copy(kv_hbm.at[inv_ref[t], :, pl.ds(h * 256, 256)],
                                     kv_s.at[h, pl.ds(t * 128, 128)], sems.at[h, t])

    @pl.when(head == 0)
    def _():
        for h in range(heads):
            for t in range(spans):
                load(h, t).start()

    for h in range(heads):
        @pl.when(head == h)
        def _():
            for t in range(spans):
                load(h, t).wait()

    dk_s[...] = jnp.zeros_like(dk_s)
    dv_s[...] = jnp.zeros_like(dv_s)

    def span(qi, q_ref, dy_ref, x_ref, y_ref, dq_ref):
        t = tq_ref[qi]
        q = stack_heads(q_ref[...])
        dy = stack_heads(dy_ref[...])
        rows = q.shape[0]
        blocks = (t * 128) // block
        short = t * 128 + 128 - blocks * block <= small

        def forward(b, size, masked, carry):
            m, l, acc = carry
            at = pl.multiple_of(b * block, block)
            k = kv_s[head, pl.ds(at, size), 0:128]
            v = kv_s[head, pl.ds(at, size), 128:256]
            s = lax.dot_general(k, q, NT, preferred_element_type=F32)
            if masked:
                kpos = at + lax.broadcasted_iota(jnp.int32, (size, 128), 0)
                qpos = t * 128 + lax.broadcasted_iota(jnp.int32, (size, 128), 1)
                visible = kpos <= qpos
                s = jnp.concatenate([jnp.where(visible, s[:, j * 128:(j + 1) * 128], -1e30) for j in range(8)], 1)
            m_new = jnp.maximum(m, jnp.max(s, 0, keepdims=True))
            e = jnp.exp2((s - m_new) * c)
            fade = jnp.exp2((m - m_new) * c)
            rounded = e.astype(BF)
            e_s[pl.ds(at, size), :] = rounded
            top_s[b] = jnp.broadcast_to(m_new, (8, rows))
            l = l * fade + jnp.sum(e, 0, keepdims=True)
            acc = acc * fade + lax.dot_general(v, rounded, TN, preferred_element_type=F32)
            return m_new, l, acc

        def over_blocks(step, carry):
            carry = lax.fori_loop(0, blocks, lambda b, cr: step(b, block, False, cr), carry)
            return lax.cond(short, lambda cr: step(blocks, small, True, cr), lambda cr: step(blocks, block, True, cr), carry)

        start = (jnp.full((1, rows), -1e30, F32), jnp.zeros((1, rows), F32), jnp.zeros((128, rows), F32))
        m, l, acc = over_blocks(forward, start)
        mixed = acc / l
        delta = jnp.sum(jnp.transpose(dy.astype(F32)) * mixed, 0, keepdims=True)
        y_ref[...] = (x_ref[...].astype(F32) + spread_heads(jnp.transpose(mixed))).astype(y_ref.dtype)

        def backward(b, size, masked, dq):
            at = pl.multiple_of(b * block, block)
            k = kv_s[head, pl.ds(at, size), 0:128]
            v = kv_s[head, pl.ds(at, size), 128:256]
            p = e_s[pl.ds(at, size), :].astype(F32) * (jnp.exp2((top_s[b, 0:1] - m) * c) / l)
            dp = lax.dot_general(v, dy, NT, preferred_element_type=F32)
            ds = (p * (dp - delta)).astype(BF)
            dv_s[pl.ds(at, size)] += jnp.dot(p.astype(BF), dy, preferred_element_type=F32)
            dk_s[pl.ds(at, size)] += jnp.dot(ds, q, preferred_element_type=F32)
            return dq + lax.dot_general(k, ds, TN, preferred_element_type=F32)

        dq = over_blocks(backward, jnp.zeros((128, rows), F32))
        dq_ref[...] = spread_heads(jnp.transpose(dq * scale)).astype(dq_ref.dtype)

    span(0, q_own, dy_own, x_own, y_own, dq_own)
    span(1, q_got, dy_got, x_got, y_got, dq_got)
    for t in range(spans):
        at = pl.ds(pl.multiple_of(inv_ref[t] * 128, 128), 128)
        terms_ref[at, 0:128] = (dk_s[t * 128:(t + 1) * 128] * scale).astype(BF)
        terms_ref[at, 128:256] = dv_s[t * 128:(t + 1) * 128].astype(BF)


def attention(q, dy, x, kv, tq, inv, block=1024, small=512):
    spans = kv.shape[0]
    count = kv.shape[2] // 256
    own = pl.BlockSpec((128, 1024), lambda h, tq, inv: (0, tq[2] * count + h))
    got = pl.BlockSpec((128, 1024), lambda h, tq, inv: (0, h))
    flops = 2 * 7 * 2 * count * 1024 * spans * 128 * 128
    rows = jax.ShapeDtypeStruct((128, count * 1024), BF)
    return pl.pallas_call(
        functools.partial(attention_kernel, block, small),
        grid_spec=pltpu.PrefetchScalarGridSpec(
            num_scalar_prefetch=2,
            grid=(count,),
            in_specs=[own, got] * 3 + [pl.BlockSpec(memory_space=pl.ANY)],
            out_specs=[got] * 4 + [pl.BlockSpec((spans * 128, 256), lambda h, tq, inv: (0, h))],
            scratch_shapes=[pltpu.VMEM((count, spans * 128, 256), BF), pltpu.VMEM((spans * 128, 128), F32),
                            pltpu.VMEM((spans * 128, 128), F32), pltpu.VMEM((spans * 128, 1024), BF),
                            pltpu.VMEM((spans * 128 // block, 8, 1024), F32), pltpu.SemaphoreType.DMA((count, spans))],
        ),
        out_shape=[rows] * 4 + [jax.ShapeDtypeStruct((spans * 128, count * 256), BF)],
        compiler_params=pltpu.CompilerParams(vmem_limit_bytes=50 << 20),
        cost_estimate=pl.CostEstimate(flops=flops, bytes_accessed=16 << 20, transcendentals=0),
        name="attention",
    )(tq, inv, *q, *dy, *x, kv)


MESH_ID = pl.DeviceIdType.MESH
EPS = 1e-05
DOWN, UP = 0, 1
OWN, PAIR = 0, 1
UNITS = [(UP, OWN), (UP, PAIR), (DOWN, OWN), (DOWN, PAIR)]


class Place:
    def __init__(self):
        self.me = lax.axis_index("ctx")
        self.core = self.me % 2
        self.chip = self.me // 2
        beside = self.chip % 2
        self.partner = self.me + 1 - 2 * self.core
        self.across = self.me + 2 - 4 * beside
        self.above = (self.me + 4) % 16
        self.below = (self.me + 12) % 16
        self.chip_x = self.chip + 1 - 2 * beside

    def greet_all(self, barrier):
        for step in range(1, 16):
            pl.semaphore_signal(barrier, inc=1, device_id={"ctx": (self.me + step) % 16}, device_id_type=MESH_ID)
        mirrored = 7 - lax.axis_index("section")
        pl.semaphore_signal(barrier, inc=1, device_id={"section": mirrored}, device_id_type=MESH_ID)
        pl.semaphore_wait(barrier, 16)

    def greet(self, barrier):
        for dev in (self.partner, self.across, self.above, self.below):
            pl.semaphore_signal(barrier, inc=1, device_id={"ctx": dev}, device_id_type=MESH_ID)
        pl.semaphore_wait(barrier, 4)

    def span(self, chip, kind):
        return 2 * chip + (self.core if kind == OWN else 1 - self.core)

    def up(self, chip, by):
        return (chip + 2 * by) % 8


class Wires:
    def __init__(self, send_sem, recv_sem):
        self.send_sem, self.recv_sem, self.started = send_sem, recv_sem, []

    def copy(self, index, src, dst, dev):
        return pltpu.make_async_remote_copy(
            src_ref=src, dst_ref=dst, send_sem=self.send_sem.at[index], recv_sem=self.recv_sem.at[index],
            device_id={"ctx": dev}, device_id_type=MESH_ID)

    def send(self, index, src, dst, dev):
        copy = self.copy(index, src, dst, dev)
        copy.start()
        self.started.append(copy)

    def far_send(self, index, src, dst, section):
        copy = pltpu.make_async_remote_copy(
            src_ref=src, dst_ref=dst, send_sem=self.send_sem.at[index], recv_sem=self.recv_sem.at[index],
            device_id={"section": section}, device_id_type=MESH_ID)
        copy.start()
        self.started.append(copy)
        return copy

    def arrive(self, index, ref, dev):
        self.copy(index, ref, ref, dev).wait_recv()

    def finish(self):
        for copy in self.started:
            copy.wait_send()


X, ZM, ZP, XZM, XZP, AN, XA = range(7)


def gather_first(place, wires, base, unit, src, slot):
    kind = unit[1]
    at = base + 7 * UNITS.index(unit)
    here = slot(unit, place.chip)
    wires.send(at + X, src, here, place.across)
    wires.send(at + ZM, src, here, place.above)
    wires.send(at + ZP, src, here, place.below)


def gather_second(place, wires, base, unit, slot, landed):
    at = base + 7 * UNITS.index(unit)
    lo, hi = slot(unit, place.up(place.chip, 3)), slot(unit, place.up(place.chip, 1))
    wires.arrive(at + ZM, lo, place.below)
    if unit[1] == OWN:
        wires.send(at + AN, lo, lo, place.above)
    wires.arrive(at + ZP, hi, place.above)
    if unit[1] == PAIR:
        wires.send(at + AN, hi, hi, place.below)
    landed(unit, place.up(place.chip, 3))
    landed(unit, place.up(place.chip, 1))


def gather_third(place, wires, base, unit, slot, landed):
    at = base + 7 * UNITS.index(unit)
    far = slot(unit, place.up(place.chip, 2))
    wires.arrive(at + AN, far, place.below if unit[1] == OWN else place.above)
    wires.send(at + XA, far, far, place.across)
    cx = slot(unit, place.chip_x)
    wires.arrive(at + X, cx, place.across)
    wires.send(at + XZM, cx, cx, place.above)
    wires.send(at + XZP, cx, cx, place.below)
    landed(unit, place.up(place.chip, 2))
    landed(unit, place.chip_x)


def gather_last(place, wires, base, unit, slot, landed):
    at = base + 7 * UNITS.index(unit)
    for kind, by, dev in ((XZM, 3, place.below), (XZP, 1, place.above), (XA, 2, place.across)):
        chip = place.up(place.chip_x, by)
        wires.arrive(at + kind, slot(unit, chip), dev)
        landed(unit, chip)


def nothing(unit, chip):
    pass


def spread_kernel(act_d, act_u, cot_d, cot_u, x_d, x_u, kv_d, kv_u,
                  q_d, q_u, dy_d, dy_u, xh_d, xh_u, all_d, all_u, send_sem, recv_sem, local_sem):
    place = Place()
    wires = Wires(send_sem, recv_sem)
    place.greet(pltpu.get_barrier_semaphore())
    all_kv, kv = (all_d, all_u), (kv_d, kv_u)
    mine = pl.ds(pl.multiple_of(place.core * 512, 512), 512)
    other = lambda width: pl.ds(pl.multiple_of((1 - place.core) * width, width), width)
    slot = lambda unit, chip: all_kv[unit[0]].at[place.span(chip, unit[1])]
    local = []
    for layer in (UP, DOWN):
        wires.send(28 + layer, kv[layer].at[:, other(512)], all_kv[layer].at[place.me], place.partner)
    for layer in (UP, DOWN):
        gather_first(place, wires, 0, (layer, OWN), kv[layer].at[:, mine], slot)
        copy = pltpu.make_async_copy(kv[layer].at[:, mine], all_kv[layer].at[place.me], local_sem.at[layer])
        copy.start()
        local.append(copy)
    for layer in (UP, DOWN):
        wires.arrive(28 + layer, all_kv[layer].at[place.partner], place.partner)
        gather_first(place, wires, 0, (layer, PAIR), slot((layer, PAIR), place.chip), slot)
    halves = ((act_u, q_u), (cot_u, dy_u), (x_u, xh_u), (act_d, q_d), (cot_d, dy_d), (x_d, xh_d))
    for n, (src, dst) in enumerate(halves):
        wires.send(30 + n, src.at[:, other(2048)], dst, place.partner)
    for unit in UNITS:
        gather_second(place, wires, 0, unit, slot, nothing)
    for unit in UNITS:
        gather_third(place, wires, 0, unit, slot, nothing)
    for unit in UNITS:
        gather_last(place, wires, 0, unit, slot, nothing)
    for n, (src, dst) in enumerate(halves):
        wires.arrive(30 + n, dst, place.partner)
    for copy in local:
        copy.wait()
    wires.finish()


def spread(*operands):
    half = jax.ShapeDtypeStruct((128, 2048), BF)
    hbm = pl.BlockSpec(memory_space=pl.ANY)
    return pl.pallas_call(
        spread_kernel,
        in_specs=[hbm] * 6 + [pl.BlockSpec(memory_space=pltpu.VMEM)] * 2,
        out_specs=[hbm] * 8,
        out_shape=[half] * 6 + [jax.ShapeDtypeStruct((16, 128, 512), BF)] * 2,
        scratch_shapes=[pltpu.SemaphoreType.DMA((36,)), pltpu.SemaphoreType.DMA((36,)), pltpu.SemaphoreType.DMA((2,))],
        compiler_params=pltpu.CompilerParams(collective_id=1, has_side_effects=True),
        name="spread",
    )(*operands)


R0, RA, RB, R1, RU, RD, RX = range(7)


HANDED, DQ, GAINS, FAR = 56, 88, 90, 120


def finish_kernel(terms_d, parts_u, dqo_d, dqo_u, dqg_d, dqg_u, x_d, x_u, cot_d, cot_u, act_hbm, weights, gains,
                  grad_d, grad_u, kv_grad, gain_grad,
                  slots, stage, total, all_kv, dquery, weight, dact, gparts, ggot, gsum, acc, wsend, wgot, ggot_far,
                  kept, parts, x_s, cot_s, features, grad_s, send_sem, recv_sem, local_sem):
    place = Place()
    wires = Wires(send_sem, recv_sem)
    mirrored = 7 - lax.axis_index("section")
    chip, chip_x = place.chip, place.chip_x
    local = []

    def keep(src, dst):
        copy = pltpu.make_async_copy(src, dst, local_sem.at[len(local)])
        copy.start()
        local.append(copy)
        return copy

    loads = {}
    loads["terms"], loads["parts"] = keep(terms_d, kept), keep(parts_u, parts)
    place.greet_all(pltpu.get_barrier_semaphore())

    def rows(unit, at):
        return pl.ds(pl.multiple_of(place.span(at, unit[1]) * 128, 128), 128)

    def sent(unit, at):
        return terms_d.at[rows(unit, at)]

    def term(unit, at):
        return kept.at[rows(unit, at)]

    def plus(*refs):
        value = refs[0][...].astype(F32)
        for ref in refs[1:]:
            value = value + ref[...].astype(F32)
        return value.astype(BF)

    def reduce_first(layer):
        for n, unit in enumerate(UNITS):
            if unit[0] == layer:
                at = 7 * n
                wires.send(at + R0, sent(unit, place.up(chip_x, 2)), slots.at[at + R0], place.across)
                wires.send(at + RA, sent(unit, place.up(chip_x, 1)), slots.at[at + RA], place.above)
                wires.send(at + RB, sent(unit, place.up(chip_x, 3)), slots.at[at + RB], place.below)

    def reduce_second(layer):
        for n, unit in enumerate(UNITS):
            if unit[0] == layer:
                at = 7 * n
                wires.arrive(at + R0, slots.at[at + R0], place.across)
                stage[3 * n] = plus(slots.at[at + R0], term(unit, place.up(chip, 2)))
                wires.send(at + R1, stage.at[3 * n], slots.at[at + R1], place.below if unit[1] == OWN else place.above)

    def reduce_direct(layer):
        for n, unit in enumerate(UNITS):
            if unit[0] == layer:
                at = 7 * n
                if unit[1] == OWN:
                    wires.send(at + RD, sent(unit, place.up(chip, 1)), slots.at[at + RD], place.above)
                else:
                    wires.send(at + RU, sent(unit, place.up(chip, 3)), slots.at[at + RU], place.below)

    def reduce_third(layer):
        for n, unit in enumerate(UNITS):
            if unit[0] == layer:
                at = 7 * n
                wires.arrive(at + RA, slots.at[at + RA], place.below)
                wires.arrive(at + RB, slots.at[at + RB], place.above)
                stage[3 * n + 1] = plus(slots.at[at + RA], slots.at[at + RB], term(unit, chip_x))
                wires.send(at + RX, stage.at[3 * n + 1], slots.at[at + RX], place.across)
        for n, unit in enumerate(UNITS):
            if unit[0] == layer:
                at = 7 * n
                if unit[1] == OWN:
                    wires.arrive(at + R1, slots.at[at + R1], place.above)
                    stage[3 * n + 2] = plus(slots.at[at + R1], term(unit, place.up(chip, 3)))
                    wires.send(at + RU, stage.at[3 * n + 2], slots.at[at + RU], place.below)
                else:
                    wires.arrive(at + R1, slots.at[at + R1], place.below)
                    stage[3 * n + 2] = plus(slots.at[at + R1], term(unit, place.up(chip, 1)))
                    wires.send(at + RD, stage.at[3 * n + 2], slots.at[at + RD], place.above)

    def load_rest(layer, own_part, other_part, x_ref, cot_ref):
        wires.send(DQ + layer, other_part, dquery.at[layer, place.core], place.partner)
        loads["rest", layer] = [
            keep(own_part, dquery.at[layer, place.core]), keep(x_ref, x_s.at[layer]), keep(cot_ref, cot_s.at[layer]),
            keep(weights.at[1 if layer == UP else 0, 0], weight.at[layer])]

    slot = lambda unit, at: all_kv.at[unit[0], place.core, place.span(at, unit[1])]
    order = []

    def landed(unit, at):
        ref = slot(unit, at)
        wires.send(HANDED + len(order), ref, ref, place.partner)
        order.append((unit, at))

    def spread_total(n, unit):
        gather_first(place, wires, 28, unit, total.at[n], slot)
        all_kv[unit[0], place.core, place.span(chip, unit[1])] = total[n]
        wires.send(HANDED + len(order), total.at[n], slot(unit, chip), place.partner)
        order.append((unit, chip))

    def reduce_last(layer):
        for n, unit in enumerate(UNITS):
            if unit[0] == layer:
                at = 7 * n
                wires.arrive(at + RX, slots.at[at + RX], place.across)
                wires.arrive(at + RU, slots.at[at + RU], place.above)
                wires.arrive(at + RD, slots.at[at + RD], place.below)
                total[n] = plus(slots.at[at + RX], slots.at[at + RU], slots.at[at + RD], term(unit, chip))
                spread_total(n, unit)

    def add_parts(layer):
        for n, unit in enumerate(UNITS):
            if unit[0] == layer:
                here = pl.ds(pl.multiple_of((place.core if unit[1] == OWN else 1 - place.core) * 128, 128), 128)
                total[n] = plus(*[parts.at[came, here] for came in range(8)])
                spread_total(n, unit)

    waited = set()

    def handed(chosen):
        for n, (unit, at) in enumerate(order):
            if chosen(unit, at) and n not in waited:
                waited.add(n)
                ref = all_kv.at[unit[0], 1 - place.core, place.span(at, 1 - unit[1])]
                wires.arrive(HANDED + n, ref, place.partner)

    def complete(layer, grad_ref):
        handed(lambda unit, at: unit[0] == layer and at is chip)
        for copy in loads["rest", layer]:
            copy.wait()
        wires.arrive(DQ + layer, dquery.at[layer, 1 - place.core], place.partner)
        halves = [all_kv[layer, half, place.me] for half in range(2)]
        dkv = jnp.concatenate([halves[h // 2][:, (h % 2) * 256 + kind * 128:(h % 2) * 256 + kind * 128 + 128]
                               for kind in range(2) for h in range(4)], 1)
        total_sq = jnp.zeros((128, 1), F32)
        for tile in range(8):
            part = x_s[layer, :, tile * 512:(tile + 1) * 512].astype(F32)
            total_sq = total_sq + jnp.sum(part * part, 1, keepdims=True)
        recip = lax.rsqrt(total_sq / 4096 + EPS)

        def first(tile, dots):
            cols = pl.ds(pl.multiple_of(tile * 512, 512), 512)
            normed = x_s[layer, :, cols].astype(F32) * recip
            within = pl.ds(pl.multiple_of(tile % 4 * 512, 512), 512)
            value = dquery[layer, tile // 4, :, within].astype(F32) + lax.dot_general(
                dkv, weight[layer, cols, :], NT, preferred_element_type=F32)
            dact[:, cols] = value
            product = value * normed
            column = jnp.sum(product, 0, keepdims=True)
            for half in range(2):
                gparts[layer, 2 * tile + half] = jnp.broadcast_to(column[:, half * 256:(half + 1) * 256], (8, 256))
            return dots + jnp.sum(product * gains[layer:layer + 1, cols], 1, keepdims=True)

        dots = lax.fori_loop(0, 8, first, jnp.zeros((128, 1), F32))
        for step in range(1, 16):
            to = (place.me + step) % 16
            wires.send(GAINS + 15 * layer + step - 1, gparts.at[layer, to], ggot.at[layer, step], to)
        mean = dots / 4096

        def second(tile, _):
            cols = pl.ds(pl.multiple_of(tile * 512, 512), 512)
            normed = x_s[layer, :, cols].astype(F32) * recip
            dnormed = dact[:, cols] * gains[layer:layer + 1, cols]
            grad_s[layer, :, cols] = (cot_s[layer, :, cols].astype(F32) + recip * (dnormed - normed * mean)).astype(BF)
            return 0

        lax.fori_loop(0, 8, second, 0)
        loads["grad", layer] = keep(grad_s.at[layer], grad_ref)

    def gain_total(layer):
        value = gparts[layer, place.me]
        for step in range(1, 16):
            wires.arrive(GAINS + 15 * layer + step - 1, ggot.at[layer, step], (place.me + step) % 16)
            value = value + ggot[layer, step]
        return value

    def weight_grad(layer):
        acc[...] = jnp.zeros_like(acc)

        def step(n, _):
            two = pl.ds(2 * n, 2)
            act = features[two, layer].reshape(256, 256)
            for half in range(2):
                dkv = all_kv[layer, half, two].reshape(256, 512)
                acc[:, half * 512:(half + 1) * 512] += lax.dot_general(act, dkv, TN, preferred_element_type=F32)
            return 0

        lax.fori_loop(0, 8, step, 0)

    def stage_of(step, layer):
        for unit in UNITS:
            if unit[0] == layer:
                step(place, wires, 28, unit, slot, landed)

    reduce_first(DOWN)
    loads["parts"].wait()
    add_parts(UP)
    loads["terms"].wait()
    load_rest(UP, dqo_u, dqg_u, x_u, cot_u)
    reduce_second(DOWN)
    load_rest(DOWN, dqo_d, dqg_d, x_d, cot_d)
    loads["act"] = keep(act_hbm, features)
    reduce_third(DOWN)
    reduce_direct(DOWN)
    stage_of(gather_second, UP)
    reduce_last(DOWN)
    stage_of(gather_third, UP)
    stage_of(gather_second, DOWN)
    complete(UP, grad_u)
    stage_of(gather_third, DOWN)
    stage_of(gather_last, UP)
    handed(lambda unit, at: unit[0] == UP)
    loads["act"].wait()
    weight_grad(UP)
    wsend[...] = acc[...].astype(BF)
    far_w = wires.far_send(FAR, wsend, wgot, mirrored)
    complete(DOWN, grad_d)
    gsum[...] = gain_total(UP)
    far_g = wires.far_send(FAR + 1, gsum, ggot_far, mirrored)
    stage_of(gather_last, DOWN)
    handed(lambda unit, at: True)
    weight_grad(DOWN)
    mine = gain_total(DOWN)
    far_g.wait_recv()
    gain_grad[...] = mine + ggot_far[...]
    far_w.wait_recv()
    for h in range(4):
        for kind in range(2):
            came = slice(h * 256 + kind * 128, h * 256 + kind * 128 + 128)
            goes = slice(kind * 512 + h * 128, kind * 512 + h * 128 + 128)
            kv_grad[:, goes] = acc[:, came] + wgot[:, came].astype(F32)
    for layer in (UP, DOWN):
        loads["grad", layer].wait()
    wires.finish()


def finish(*operands):
    hbm = pl.BlockSpec(memory_space=pl.ANY)
    vmem = pl.BlockSpec(memory_space=pltpu.VMEM)
    row = jax.ShapeDtypeStruct((128, 4096), BF)
    unit = lambda count: pltpu.VMEM((count, 128, 512), BF)
    return pl.pallas_call(
        finish_kernel,
        in_specs=[hbm] * 12 + [vmem],
        out_specs=[hbm] * 2 + [vmem] * 2,
        out_shape=[row, row, jax.ShapeDtypeStruct((256, 1024), F32), jax.ShapeDtypeStruct((8, 256), F32)],
        scratch_shapes=[unit(28), unit(12), unit(4), pltpu.VMEM((2, 2, 16, 128, 512), BF), pltpu.VMEM((2, 2, 128, 2048), BF),
                        pltpu.VMEM((2, 4096, 1024), BF), pltpu.VMEM((128, 4096), F32), pltpu.VMEM((2, 16, 8, 256), F32),
                        pltpu.VMEM((2, 16, 8, 256), F32), pltpu.VMEM((8, 256), F32), pltpu.VMEM((256, 1024), F32),
                        pltpu.VMEM((256, 1024), BF), pltpu.VMEM((256, 1024), BF), pltpu.VMEM((8, 256), F32),
                        pltpu.VMEM((2048, 512), BF), pltpu.VMEM((8, 256, 512), BF), pltpu.VMEM((2, 128, 4096), BF), pltpu.VMEM((2, 128, 4096), BF),
                        pltpu.VMEM((16, 2, 128, 256), BF), pltpu.VMEM((2, 128, 4096), BF),
                        pltpu.SemaphoreType.DMA((122,)), pltpu.SemaphoreType.DMA((122,)), pltpu.SemaphoreType.DMA((13,))],
        compiler_params=pltpu.CompilerParams(collective_id=2, has_side_effects=True, vmem_limit_bytes=60 << 20),
        name="finish",
    )(*operands)


def by_head(kv):
    return kv.reshape(-1, 2, 4, 128).transpose(0, 2, 1, 3).reshape(-1, 1024)


def prepare(x, gain, weight):
    xf = x.astype(F32)
    recip = lax.rsqrt(jnp.mean(xf * xf, -1, keepdims=True) + EPS)
    normed = xf * recip
    act = (normed * gain[None, :]).astype(BF)
    kv = jnp.dot(act, weight, preferred_element_type=F32).astype(BF)
    return act, by_head(kv)


def halves_joined(core, mine, other):
    both = jnp.concatenate([other, other], 1)
    return lax.dynamic_update_slice(both, mine, (0, core * mine.shape[1]))


def relayed(own, got, by):
    sections, spans = lax.axis_size("section"), lax.axis_size("ctx")
    to = lambda flip: [(s * spans + i, (s + by) % sections * spans + (i ^ flip)) for s in range(sections) for i in range(spans)]
    mine = lax.ppermute(own, ("section", "ctx"), to(0))
    other = lax.ppermute(got, ("section", "ctx"), to(1))
    return mine, other


def per_device(down_in, up_in, down_cot, up_cot, kv_weight, norm_gain, span_ids):
    own = lax.axis_index("ctx")
    core = own % 2
    x_d, x_u, cot_d, cot_u = down_in[0], up_in[0], down_cot[0], up_cot[0]
    gain_d, gain_u = norm_gain[0, 0], norm_gain[1, 0]
    weight_d, weight_u = kv_weight[0, 0], kv_weight[1, 0]
    scalars = jnp.stack([span_ids[own], span_ids[own + 1 - 2 * core], core]).astype(jnp.int32)
    order = jnp.arange(16, dtype=jnp.int32)
    inverse = jnp.sum(jnp.where(span_ids[:, None] == order[None, :], order[:, None], 0), 0).astype(jnp.int32)
    act_u, kv_u = prepare(x_u, gain_u, weight_u)
    act_d, kv_d = prepare(x_d, gain_d, weight_d)
    q_d, q_u, dy_d, dy_u, xh_d, xh_u, all_d, all_u = spread(act_d, act_u, cot_d, cot_u, x_d, x_u, kv_d, kv_u)
    after_d, after_u, _ = lax.optimization_barrier((act_d, act_u, q_d))
    features = jnp.stack([after_d, after_u]).reshape(2, 128, 16, 256).transpose(2, 0, 1, 3)
    features = lax.all_to_all(features, "ctx", 0, 0, tiled=False)
    yo_u, yg_u, dqo_u, dqg_u, terms_u = attention((act_u, q_u), (cot_u, dy_u), (x_u, xh_u), all_u, scalars, inverse)
    same_core = [list(range(c, 16, 2)) for c in range(2)]
    parts_u = lax.all_to_all(terms_u.reshape(8, 256, 512), "ctx", 0, 0, axis_index_groups=same_core, tiled=False)
    up_halves = relayed(yo_u, yg_u, -1)
    yo_d, yg_d, dqo_d, dqg_d, terms_d = attention((act_d, q_d), (cot_d, dy_d), (x_d, xh_d), all_d, scalars, inverse)
    down_halves = relayed(yo_d, yg_d, 1)
    grad_d, grad_u, kv_grad, gain_grad = finish(
        terms_d, parts_u, dqo_d, dqo_u, dqg_d, dqg_u, x_d, x_u, cot_d, cot_u, features, kv_weight, norm_gain[:, 0])
    down_halves, up_halves, gain_grad = lax.optimization_barrier((down_halves, up_halves, gain_grad))
    down_out, up_out = halves_joined(core, *down_halves), halves_joined(core, *up_halves)
    return (down_out[None], up_out[None], grad_d[None], grad_u[None], kv_grad[None], gain_grad[:1])


def solution(mesh):
    row = P("section", "ctx", None)
    in_specs = (row, row, row, row, P(None, "section", None, None), P(None, "section", None), P())
    out_specs = (row, row, row, row, row, P("section", "ctx"))
    return jax.shard_map(per_device, mesh=mesh, in_specs=in_specs, out_specs=out_specs, check_vma=False)
```

profile of v0, /device:TPU:1, one launch (start us, length us, event | category | flops | bytes accessed | tf_op | source)
XLA Modules:
  0.0 276.8 jit_solution(7755364803762605247)
XLA Ops:
  0.6 0.0 copy-start.10
  0.7 0.8 fusion.26
  1.5 1.5 fusion.9
  3.0 1.5 fusion.6
  4.6 0.0 copy-start.11
  4.6 0.0 copy-start.12
  4.6 4.8 %fusion.12 = bf16[128,1024]{1,0:T(8,128)(2,1)S(1)} fusion(bf16[2,1,4096,1024]{3,2,1,0:T(8,128)(2,1)} %weights.1, bf16[1,128,4096]{2,1,0:T(8,128)(2,1)S(1)} %copy-done.10, f32[4096]{0:T(1024)S(1)} %bitcast.75, f32[128]{0:T(128)S(1)} %add_rsqrt_fusion.1), kind=kOutput, calls=%fused_computation.19 | convolution fusion | flops 1075970048 | bytes 9716224 | tf_op jit(solution)/shard_map/dot_general | solution.py:579
  9.4 2.0 fusion.8
  11.4 2.4 copy-done.12
  13.8 1.4 fusion.15
  15.2 0.0 copy-start.22
  15.2 0.2 reshape.83
  15.4 0.2 copy.32
  15.6 0.9 reshape.84.kv_d
  16.4 0.2 reshape.85
  16.6 0.2 copy.31
  16.8 0.9 reshape.86.kv_u
  17.7 0.1 select_reduce_fusion.inv_ref
  17.8 0.6 fusion.27
  18.4 1.4 pad_add_fusion.tq_ref
  19.8 35.9 %spread.1 = (bf16[128,2048]{1,0:T(8,128)(2,1)}, bf16[128,2048]{1,0:T(8,128)(2,1)}, bf16[128,2048]{1,0:T(8,128)(2,1)}, bf16[128,2048]{1,0:T(8,128)(2,1)}, bf16[12...) custom-call(bf16[128,4096]{1,0:T(8,128)(2,1)} %get-tuple-element.53., ...), custom_call_target="tpu_custom_call" | custom-call | tf_op jit(solution)/shard_map/spread/pallas_call | solution.py:295
  55.7 1.0 copy-done.7
  56.7 1.0 copy-done.8
  57.7 1.0 copy-done.9
  58.8 26.5 %attention.3 = (bf16[128,2048]{1,0:T(8,128)(2,1)S(1)}, bf16[128,2048]{1,0:T(8,128)(2,1)S(1)}, bf16[128,2048]{1,0:T(8,128)(2,1)S(1)}, bf16[128,2048]{1,0:T(8,128)(2,1)S(1)}, bf16[2048,512]{1,0:T(8,128)(2,1)}) custom-call(s32[3]{0:T(128)S(1)} %pad_add_fusion.tq_ref, s32[16]{0:T(128)S(1)} %select_reduce_fusion.inv_ref, ...), custom_call_target="tpu_custom_call" | custom-call | flops 15032385536 | bytes 16777216 | tf_op jit(solution)/shard_map/attention/pallas_call | solution.py:120
  85.3 0.0 copy-start
  85.3 0.8 copy-done
  86.1 0.8 copy-done.1
  86.8 16.4 %all-to-all-start = ((bf16[8,256,512]{2,1,0:T(8,128)(2,1)}), bf16[8,256,512]{2,1,0:T(8,128)(2,1)}, u32[]{:S(2)}, u32[]{:S(2)}) async-start(bf16[8,256,512]{2,1,0:T(8,128)(2,1)} %bitcast.66), calls=%async_computation | async-start | bytes 4194304 | tf_op jit(solution)/shard_map/all_to_all | solution.py:613
  103.3 0.0 copy-start.14
  103.3 1.3 copy.23
  104.6 2.3 copy.25
  106.9 0.7 copy.24
  107.5 0.0 copy-start.15
  107.5 1.3 copy.26
  108.9 2.8 %maximum_bitcast_fusion = bf16[16,2,128,256]{3,2,1,0:T(8,128)(2,1)} fusion(bf16[1,128,16,256]{3,1,0,2:T(8,128)(2,1)} %copy.26, bf16[1,128,16,256]{3,1,0,2:T(8,128)(2,1)S(1)} %copy-done.15), kind=kLoop, calls=%fused_computation.16 | loop fusion | flops 1048576 | bytes 4194304 | tf_op jit(solution)/shard_map/transpose | solution.py:609
  111.7 16.9 %all-to-all-done.parts_u = bf16[8,256,512]{2,1,0:T(8,128)(2,1)} async-done(((bf16[8,256,512]{2,1,0:T(8,128)(2,1)}), bf16[8,256,512]{2,1,0:T(8,128)(2,1)}, u32[]{:S(2)}, u32[]{:S(2)}) %all-to-all-start) | async-done | bytes 2097184 | tf_op jit(solution)/shard_map/all_to_all | solution.py:613
  128.5 6.9 %all-to-all-start.1 = ((bf16[16,2,128,256]{3,2,1,0:T(8,128)(2,1)}), bf16[16,2,128,256]{3,2,1,0:T(8,128)(2,1)}, u32[]{:S(2)}, u32[]{:S(2)}) async-start(bf16[16,2,128,256]{3,2,1,0:T(8,128)(2,1)} %maximum_bitcast_fusion), calls=%async_computation.1 | async-start | bytes 4194304 | tf_op jit(solution)/shard_map/all_to_all | solution.py:610
  135.5 4.9 %collective-permute-start.2 = (bf16[128,2048]{1,0:T(8,128)(2,1)S(1)}, bf16[128,2048]{1,0:T(8,128)(2,1)}, u32[]{:S(2)}, u32[]{:S(2)}) collective-permute-start(bf16[128,2048]{1,0:T(8,128)(2,1)S(1)} %get-tuple-element.45), channel_id=1, source_target_pairs={{0,112},{1,113},{2,114},{3,115},{4,116},{5,117},{6,118},{7,119},{8... | collective-permute-start | bytes 1572872 | tf_op jit(solution)/shard_map/ppermute | solution.py:591
  140.4 1.0 collective-permute-start.3
  141.4 26.3 %attention.2 = (bf16[128,2048]{1,0:T(8,128)(2,1)}, bf16[128,2048]{1,0:T(8,128)(2,1)S(1)}, bf16[128,2048]{1,0:T(8,128)(2,1)S(1)}, bf16[128,2048]{1,0:T(8,128)(2,1)S(1)}, bf16[2048,512]{1,0:T(8,128)(2,1)}) custom-call(s32[3]{0:T(128)S(1)} %pad_add_fusion.tq_ref, s32[16]{0:T(128)S(1)} %select_reduce_fusion.inv_ref, ...), custom_call_target="tpu_custom_call" | custom-call | flops 15032385536 | bytes 16777216 | tf_op jit(solution)/shard_map/attention/pallas_call | solution.py:120
  167.7 0.0 copy-start.2
  167.7 0.8 copy-done.2
  168.5 0.8 copy-done.3
  169.3 1.0 collective-permute-start
  170.3 0.0 collective-permute-start.1
  170.3 0.6 copy.33
  170.9 0.0 all-to-all-done.1.act_hbm
  170.9 98.6 %finish.1 = (bf16[128,4096]{1,0:T(8,128)(2,1)}, bf16[128,4096]{1,0:T(8,128)(2,1)}, f32[256,1024]{1,0:T(8,128)}, f32[8,256]{1,0:T(8,128)}) custom-call(bf16[2048,512]{1,0:T(8,128)(2,1)} %get-tuple-element.47.terms_d, bf16[8,256,512]{2,1,0:T(8,128)(2,1)} %all-to-all-done.parts_u, bf16[128,2048]{1,0:T(8,128)(2,1)} %copy-done.2, bf16[128,2048]{1,0:T(8,128)(2,1)} %copy-done, ...), custom_call_target="tpu_custom_call" | custom-call | tf_op jit(solution)/shard_map/finish/pallas_call | solution.py:553
  269.5 0.0 collective-permute-done.2
  269.5 0.0 collective-permute-done.3
  269.5 0.0 collective-permute-done
  269.5 0.0 collective-permute-done.1
  269.5 1.3 maximum_bitcast_fusion.2
  270.8 0.1 maximum_bitcast_fusion.1
  271.0 1.3 slice.19
  272.3 1.2 bitcast_dynamic-update-slice_fusion
  273.5 0.0 copy-start.17
  273.5 0.1 bitcast_dynamic-update-slice_fusion.1
  273.6 0.0 copy-start.16
  273.6 1.0 copy.39
  274.6 1.0 copy.40
  275.6 0.1 copy-done.18
  275.6 1.0 copy.41
  (29 shorter events, 0.1 us)
Async XLA Ops:
  0.6 3.9 %copy-start.10 = (bf16[1,128,4096]{2,1,0:T(8,128)(2,1)S(1)}, bf16[1,128,4096]{2,1,0:T(8,128)(2,1)}, u32[]{:S(2)}) copy-start(bf16[1,128,4096]{2,1,0:T(8,128)(2,1)} %param.7) | copy-start | bytes 3145732
  4.6 4.9 %copy-start.11 = (bf16[1,128,4096]{2,1,0:T(8,128)(2,1)S(1)}, bf16[1,128,4096]{2,1,0:T(8,128)(2,1)}, u32[]{:S(2)}) copy-start(bf16[1,128,4096]{2,1,0:T(8,128)(2,1)} %param.8) | copy-start | bytes 3145732
  4.6 9.2 %copy-start.12 = (bf16[2,1,4096,1024]{3,2,1,0:T(8,128)(2,1)S(1)}, bf16[2,1,4096,1024]{3,2,1,0:T(8,128)(2,1)}, u32[]{:S(2)}) copy-start(bf16[2,1,4096,1024]{3,2,1,0:T(8,128)(2,1)} %weights.1) | copy-start | bytes 50331652
  15.2 2.5 copy-start.22
  55.6 1.0 copy-start.7
  56.7 1.0 copy-start.8
  57.7 1.0 copy-start.9
  85.3 0.8 copy-start
  86.0 0.8 copy-start.1
  86.8 16.4 %copy-start.13 = (bf16[128,4096]{1,0:T(8,128)(2,1)S(1)}, bf16[128,4096]{1,0:T(8,128)(2,1)}, u32[]{:S(2)}) copy-start(bf16[128,4096]{1,0:T(8,128)(2,1)} %get-tuple-element.53.act_d.q_own) | copy-start | bytes 3145732
  86.8 41.7 %all-to-all-start = ((bf16[8,256,512]{2,1,0:T(8,128)(2,1)}), bf16[8,256,512]{2,1,0:T(8,128)(2,1)}, u32[]{:S(2)}, u32[]{:S(2)}) async-start(bf16[8,256,512]{2,1,0:T(8,128)(2,1)} %bitcast.66), calls=%async_computation | async-start | bytes 4194304 | tf_op jit(solution)/shard_map/all_to_all | solution.py:613
  103.3 3.6 %copy-start.14 = (bf16[128,4096]{1,0:T(8,128)(2,1)S(1)}, bf16[128,4096]{1,0:T(8,128)(2,1)}, u32[]{:S(2)}) copy-start(bf16[128,4096]{1,0:T(8,128)(2,1)} %get-tuple-element.54.act_u.q_own) | copy-start | bytes 3145732
  107.5 1.3 copy-start.15
  111.7 29.7 %copy-start.4 = (bf16[128,2048]{1,0:T(8,128)(2,1)S(1)}, bf16[128,2048]{1,0:T(8,128)(2,1)}, u32[]{:S(2)}) copy-start(bf16[128,2048]{1,0:T(8,128)(2,1)} %get-tuple-element.35.q_got) | copy-start | bytes 1572868
  111.7 29.7 %copy-start.5 = (bf16[128,2048]{1,0:T(8,128)(2,1)S(1)}, bf16[128,2048]{1,0:T(8,128)(2,1)}, u32[]{:S(2)}) copy-start(bf16[128,2048]{1,0:T(8,128)(2,1)} %get-tuple-element.36.dy_got) | copy-start | bytes 1572868
  111.7 29.7 %copy-start.6 = (bf16[128,2048]{1,0:T(8,128)(2,1)S(1)}, bf16[128,2048]{1,0:T(8,128)(2,1)}, u32[]{:S(2)}) copy-start(bf16[128,2048]{1,0:T(8,128)(2,1)} %get-tuple-element.37.x_got) | copy-start | bytes 1572868
  128.5 42.4 %all-to-all-start.1 = ((bf16[16,2,128,256]{3,2,1,0:T(8,128)(2,1)}), bf16[16,2,128,256]{3,2,1,0:T(8,128)(2,1)}, u32[]{:S(2)}, u32[]{:S(2)}) async-start(bf16[16,2,128,256]{3,2,1,0:T(8,128)(2,1)} %maximum_bitcast_fusion), calls=%async_computation.1 | async-start | bytes 4194304 | tf_op jit(solution)/shard_map/all_to_all | solution.py:610
  135.5 134.0 %collective-permute-start.2 = (bf16[128,2048]{1,0:T(8,128)(2,1)S(1)}, bf16[128,2048]{1,0:T(8,128)(2,1)}, u32[]{:S(2)}, u32[]{:S(2)}) collective-permute-start(bf16[128,2048]{1,0:T(8,128)(2,1)S(1)} %get-tuple-element.45), channel_id=1, source_target_pairs={{0,112},{1,113},{2,114},{3,115},{4,116},{5,117},{6,118},{7,119},{8... | collective-permute-start | bytes 1572872 | tf_op jit(solution)/shard_map/ppermute | solution.py:591
  140.4 129.1 %collective-permute-start.3 = (bf16[128,2048]{1,0:T(8,128)(2,1)S(1)}, bf16[128,2048]{1,0:T(8,128)(2,1)}, u32[]{:S(2)}, u32[]{:S(2)}) collective-permute-start(bf16[128,2048]{1,0:T(8,128)(2,1)S(1)} %get-tuple-element.46), channel_id=1, source_target_pairs={{0,113},{1,112},{2,115},{3,114},{4,117},{5,116},{6,119},{7,118},{8... | collective-permute-start | bytes 1572872 | tf_op jit(solution)/shard_map/ppermute | solution.py:592
  141.4 28.9 %copy-start.21 = (f32[2,1,4096]{2,1,0:T(1,128)S(1)}, f32[2,1,4096]{2,1,0:T(1,128)}, u32[]{:S(2)}) copy-start(f32[2,1,4096]{2,1,0:T(1,128)} %param.12) | copy-start | bytes 98308
  167.7 0.8 copy-start.2
  168.5 0.8 copy-start.3
  169.3 100.3 %collective-permute-start = (bf16[128,2048]{1,0:T(8,128)(2,1)}, bf16[128,2048]{1,0:T(8,128)(2,1)S(1)}, u32[]{:S(2)}, u32[]{:S(2)}) collective-permute-start(bf16[128,2048]{1,0:T(8,128)(2,1)} %get-tuple-element.39), channel_id=1, source_target_pairs={{0,16},{1,17},{2,18},{3,19},{4,20},{5,21},{6,22},{7,23},{8,24},{9,... | collective-permute-start | bytes 1572872 | tf_op jit(solution)/shard_map/ppermute | solution.py:591
  170.3 99.3 %collective-permute-start.1 = (bf16[128,2048]{1,0:T(8,128)(2,1)S(1)}, bf16[128,2048]{1,0:T(8,128)(2,1)S(1)}, u32[]{:S(2)}, u32[]{:S(2)}) collective-permute-start(bf16[128,2048]{1,0:T(8,128)(2,1)S(1)} %get-tuple-element.40), channel_id=1, source_target_pairs={{0,17},{1,16},{2,19},{3,18},{4,21},{5,20},{6,23},{7,22},{8,25},{9,... | collective-permute-start | bytes 1572872 | tf_op jit(solution)/shard_map/ppermute | solution.py:592
  270.8 2.7 copy-start.20
  272.3 2.3 copy-start.19
  273.5 2.1 copy-start.17
  273.6 2.0 copy-start.16
  273.6 2.0 copy-start.18
where the time goes:
time: 282 us; the launch traced here: 277 us
  Pallas kernels  187 us (66%)
  starting transfers between devices  30.3 us (11%)
  local copies, waits for them, and re-layouts  24.4 us (9%)
  waiting for transfers between devices  16.9 us (6%)
  other arithmetic  10.7 us (4%)
  matrix products  6.19 us (2%)
    pallas_call x1, Pallas kernels, finish(): pl.pallas_call(finish_kernel, in_specs=[hbm] * 12 + [vmem], out_specs=[hb...  98.6 us
    pallas_call x2, Pallas kernels, attention(): pl.pallas_call(functools.partial(attention_kernel, block, small), grid_sp...  52.8 us
    pallas_call x1, Pallas kernels, spread(): pl.pallas_call(spread_kernel, in_specs=[hbm] * 6 + [pl.BlockSpec(memory_s...  35.9 us
    all_to_all x1, waiting for transfers between devices, per_device(): lax.all_to_all(terms_u.reshape(8, 256, 512), 'ctx', 0, 0, axis_index_grou...  16.9 us
    all_to_all x1, starting transfers between devices, per_device(): lax.all_to_all(terms_u.reshape(8, 256, 512), 'ctx', 0, 0, axis_index_grou...  16.4 us
    unnamed x50, local copies, waits for them, and re-layouts  12.4 us
    all_to_all x1, starting transfers between devices, per_device(): features = lax.all_to_all(features, 'ctx', 0, 0, tiled=False)  6.94 us
    dot_general x2, matrix products, prepare(): kv = jnp.dot(act, weight, preferred_element_type=F32).astype(BF)  6.19 us
  transfers between devices with their start and end apart: 6, of which 1 were waited for; matrix products, arithmetic and copies ran while one was open for 3% of the time, Pallas kernels for 45%

commit v1 on v0

--- a/solution.py
+++ b/solution.py
@@ -129,7 +129,7 @@
                             pltpu.VMEM((spans * 128 // block, 8, 1024), F32), pltpu.SemaphoreType.DMA((count, spans))],
         ),
         out_shape=[rows] * 4 + [jax.ShapeDtypeStruct((spans * 128, count * 256), BF)],
-        compiler_params=pltpu.CompilerParams(vmem_limit_bytes=50 << 20),
+        compiler_params=pltpu.CompilerParams(vmem_limit_bytes=60 << 20),
         cost_estimate=pl.CostEstimate(flops=flops, bytes_accessed=16 << 20, transcendentals=0),
         name="attention",
     )(tq, inv, *q, *dy, *x, kv)
@@ -254,20 +254,25 @@
 
 
 def spread_kernel(act_d, act_u, cot_d, cot_u, x_d, x_u, kv_d, kv_u,
-                  q_d, q_u, dy_d, dy_u, xh_d, xh_u, all_d, all_u, send_sem, recv_sem, local_sem):
+                  q_d, q_u, dy_d, dy_u, xh_d, xh_u, all_d, all_u, kv, send_sem, recv_sem, local_sem):
     place = Place()
     wires = Wires(send_sem, recv_sem)
+    for layer, source in ((UP, kv_u), (DOWN, kv_d)):
+        for h in range(4):
+            for kind in range(2):
+                kv[layer, :, (2 * h + kind) * 128:(2 * h + kind + 1) * 128] = (
+                    source[:, kind * 512 + h * 128:kind * 512 + (h + 1) * 128])
     place.greet(pltpu.get_barrier_semaphore())
-    all_kv, kv = (all_d, all_u), (kv_d, kv_u)
+    all_kv = (all_d, all_u)
     mine = pl.ds(pl.multiple_of(place.core * 512, 512), 512)
     other = lambda width: pl.ds(pl.multiple_of((1 - place.core) * width, width), width)
     slot = lambda unit, chip: all_kv[unit[0]].at[place.span(chip, unit[1])]
     local = []
     for layer in (UP, DOWN):
-        wires.send(28 + layer, kv[layer].at[:, other(512)], all_kv[layer].at[place.me], place.partner)
+        wires.send(28 + layer, kv.at[layer, :, other(512)], all_kv[layer].at[place.me], place.partner)
     for layer in (UP, DOWN):
-        gather_first(place, wires, 0, (layer, OWN), kv[layer].at[:, mine], slot)
-        copy = pltpu.make_async_copy(kv[layer].at[:, mine], all_kv[layer].at[place.me], local_sem.at[layer])
+        gather_first(place, wires, 0, (layer, OWN), kv.at[layer, :, mine], slot)
+        copy = pltpu.make_async_copy(kv.at[layer, :, mine], all_kv[layer].at[place.me], local_sem.at[layer])
         copy.start()
         local.append(copy)
     for layer in (UP, DOWN):
@@ -297,7 +302,7 @@
         in_specs=[hbm] * 6 + [pl.BlockSpec(memory_space=pltpu.VMEM)] * 2,
         out_specs=[hbm] * 8,
         out_shape=[half] * 6 + [jax.ShapeDtypeStruct((16, 128, 512), BF)] * 2,
-        scratch_shapes=[pltpu.SemaphoreType.DMA((36,)), pltpu.SemaphoreType.DMA((36,)), pltpu.SemaphoreType.DMA((2,))],
+        scratch_shapes=[pltpu.VMEM((2, 128, 1024), BF), pltpu.SemaphoreType.DMA((36,)), pltpu.SemaphoreType.DMA((36,)), pltpu.SemaphoreType.DMA((2,))],
         compiler_params=pltpu.CompilerParams(collective_id=1, has_side_effects=True),
         name="spread",
     )(*operands)
@@ -533,7 +538,7 @@
     weight_grad(DOWN)
     mine = gain_total(DOWN)
     far_g.wait_recv()
-    gain_grad[...] = mine + ggot_far[...]
+    gain_grad[...] = (mine + ggot_far[...])[0:1]
     far_w.wait_recv()
     for h in range(4):
         for kind in range(2):
@@ -554,7 +559,7 @@
         finish_kernel,
         in_specs=[hbm] * 12 + [vmem],
         out_specs=[hbm] * 2 + [vmem] * 2,
-        out_shape=[row, row, jax.ShapeDtypeStruct((256, 1024), F32), jax.ShapeDtypeStruct((8, 256), F32)],
+        out_shape=[row, row, jax.ShapeDtypeStruct((256, 1024), F32), jax.ShapeDtypeStruct((1, 256), F32)],
         scratch_shapes=[unit(28), unit(12), unit(4), pltpu.VMEM((2, 2, 16, 128, 512), BF), pltpu.VMEM((2, 2, 128, 2048), BF),
                         pltpu.VMEM((2, 4096, 1024), BF), pltpu.VMEM((128, 4096), F32), pltpu.VMEM((2, 16, 8, 256), F32),
                         pltpu.VMEM((2, 16, 8, 256), F32), pltpu.VMEM((8, 256), F32), pltpu.VMEM((256, 1024), F32),
@@ -567,17 +572,13 @@
     )(*operands)
 
 
-def by_head(kv):
-    return kv.reshape(-1, 2, 4, 128).transpose(0, 2, 1, 3).reshape(-1, 1024)
-
-
 def prepare(x, gain, weight):
     xf = x.astype(F32)
     recip = lax.rsqrt(jnp.mean(xf * xf, -1, keepdims=True) + EPS)
     normed = xf * recip
     act = (normed * gain[None, :]).astype(BF)
     kv = jnp.dot(act, weight, preferred_element_type=F32).astype(BF)
-    return act, by_head(kv)
+    return act, kv
 
 
 def halves_joined(core, mine, other):
@@ -604,21 +605,23 @@
     inverse = jnp.sum(jnp.where(span_ids[:, None] == order[None, :], order[:, None], 0), 0).astype(jnp.int32)
     act_u, kv_u = prepare(x_u, gain_u, weight_u)
     act_d, kv_d = prepare(x_d, gain_d, weight_d)
+    gains, act_d, act_u = lax.optimization_barrier((jnp.stack([gain_d, gain_u]), act_d, act_u))
     q_d, q_u, dy_d, dy_u, xh_d, xh_u, all_d, all_u = spread(act_d, act_u, cot_d, cot_u, x_d, x_u, kv_d, kv_u)
     after_d, after_u, _ = lax.optimization_barrier((act_d, act_u, q_d))
     features = jnp.stack([after_d, after_u]).reshape(2, 128, 16, 256).transpose(2, 0, 1, 3)
     features = lax.all_to_all(features, "ctx", 0, 0, tiled=False)
     yo_u, yg_u, dqo_u, dqg_u, terms_u = attention((act_u, q_u), (cot_u, dy_u), (x_u, xh_u), all_u, scalars, inverse)
+    features, terms_u = lax.optimization_barrier((features, terms_u))
     same_core = [list(range(c, 16, 2)) for c in range(2)]
     parts_u = lax.all_to_all(terms_u.reshape(8, 256, 512), "ctx", 0, 0, axis_index_groups=same_core, tiled=False)
     up_halves = relayed(yo_u, yg_u, -1)
     yo_d, yg_d, dqo_d, dqg_d, terms_d = attention((act_d, q_d), (cot_d, dy_d), (x_d, xh_d), all_d, scalars, inverse)
     down_halves = relayed(yo_d, yg_d, 1)
     grad_d, grad_u, kv_grad, gain_grad = finish(
-        terms_d, parts_u, dqo_d, dqo_u, dqg_d, dqg_u, x_d, x_u, cot_d, cot_u, features, kv_weight, norm_gain[:, 0])
+        terms_d, parts_u, dqo_d, dqo_u, dqg_d, dqg_u, x_d, x_u, cot_d, cot_u, features, kv_weight, gains)
     down_halves, up_halves, gain_grad = lax.optimization_barrier((down_halves, up_halves, gain_grad))
     down_out, up_out = halves_joined(core, *down_halves), halves_joined(core, *up_halves)
-    return (down_out[None], up_out[None], grad_d[None], grad_u[None], kv_grad[None], gain_grad[:1])
+    return (down_out[None], up_out[None], grad_d[None], grad_u[None], kv_grad[None], gain_grad)
 
 
 def solution(mesh):

time: 282 us -> 271 us (0.961)
  Pallas kernels: 187 us -> 218 us
  waiting for transfers between devices: 16.9 us -> 0.02 us
  starting transfers between devices: 30.3 us -> 17.4 us
  local copies, waits for them, and re-layouts: 24.4 us -> 12.7 us
    pallas_call x2, Pallas kernels: 52.8 us -> 101 us  [attention(): pl.pallas_call(functools.partial(attention_kernel, block, small), grid_sp...]
    pallas_call x1, Pallas kernels: 98.6 us -> 81.4 us  [finish(): pl.pallas_call(finish_kernel, in_specs=[hbm] * 12 + [vmem], out_specs=[hb...]
    all_to_all x1, waiting for transfers between devices: 16.9 us -> 0.01 us  [per_device(): lax.all_to_all(terms_u.reshape(8, 256, 512), 'ctx', 0, 0, axis_index_grou...]
    all_to_all x1, starting transfers between devices: 16.4 us -> 4.36 us  [per_device(): lax.all_to_all(terms_u.reshape(8, 256, 512), 'ctx', 0, 0, axis_index_grou...]
    unnamed x50 -> x36, local copies, waits for them, and re-layouts: 12.4 us -> 7.98 us
  transfers between devices with their start and end apart: 6 -> 6, of which waited for: 1 -> 0; matrix products, arithmetic and copies ran while one was open for 3% -> 1% of each run, Pallas kernels for 45% -> 68%
where the time goes in v1:
time: 271 us; the launch traced here: 267 us
  Pallas kernels  218 us (80%)
  starting transfers between devices  17.4 us (6%)
  local copies, waits for them, and re-layouts  12.7 us (5%)
  other arithmetic  10 us (4%)
  matrix products  7.65 us (3%)
    pallas_call x2, Pallas kernels, attention(): pl.pallas_call(functools.partial(attention_kernel, block, small), grid_sp...  101 us
    pallas_call x1, Pallas kernels, finish(): pl.pallas_call(finish_kernel, in_specs=[hbm] * 12 + [vmem], out_specs=[hb...  81.4 us
    pallas_call x1, Pallas kernels, spread(): pl.pallas_call(spread_kernel, in_specs=[hbm] * 6 + [pl.BlockSpec(memory_s...  36 us
    unnamed x36, local copies, waits for them, and re-layouts  7.98 us
    dot_general x2, matrix products, prepare(): kv = jnp.dot(act, weight, preferred_element_type=F32).astype(BF)  7.65 us
    all_to_all x1, starting transfers between devices, per_device(): features = lax.all_to_all(features, 'ctx', 0, 0, tiled=False)  5.83 us
  transfers between devices with their start and end apart: 6, of which 0 were waited for; matrix products, arithmetic and copies ran while one was open for 1% of the time, Pallas kernels for 68%

profile of v1, /device:TPU:1, one launch (start us, length us, event | category | flops | bytes accessed | tf_op | source)
XLA Modules:
  0.0 267.1 jit_solution(17066281701488574672)
XLA Ops:
  0.6 0.0 copy-start
  0.6 0.9 fusion.26
  1.5 1.5 fusion.6
  3.0 1.5 fusion.9
  4.6 0.0 copy-done
  4.6 0.0 copy-start.1
  4.6 0.0 copy-start.2
  4.6 5.6 %fusion.12.kv_d = bf16[128,1024]{1,0:T(8,128)(2,1)} fusion(bf16[2,1,4096,1024]{3,2,1,0:T(8,128)(2,1)} %weights.1, bf16[1,128,4096]{2,1,0:T(8,128)(2,1)S(1)} %copy-done, f32[4096]{0:T(1024)S(1)} %bitcast.67, f32[128]{0:T(128)S(1)} %add_rsqrt_fusion.1), kind=kOutput, calls=%fused_computation.19 | convolution fusion | flops 1075970048 | bytes 9716224 | tf_op jit(solution)/shard_map/dot_general | solution.py:580
  10.2 0.0 copy-done.1
  10.2 2.0 fusion.8
  12.1 1.8 copy-done.2
  13.9 2.1 fusion.15.kv_u
  16.0 0.6 pad_maximum_fusion.gains
  16.6 36.0 %spread.1 = (bf16[128,2048]{1,0:T(8,128)(2,1)}, bf16[128,2048]{1,0:T(8,128)(2,1)}, bf16[128,2048]{1,0:T(8,128)(2,1)}, bf16[128,2048]{1,0:T(8,128)(2,1)}, bf16[12...) custom-call(bf16[128,4096]{1,0:T(8,128)(2,1)} %get-tuple-element.55., ...), custom_call_target="tpu_custom_call" | custom-call | tf_op jit(solution)/shard_map/spread/pallas_call | solution.py:300
  52.7 0.0 copy-done.4
  52.7 0.0 copy-start.3
  52.7 0.7 copy.18
  53.3 1.3 copy.20
  54.7 0.0 copy-done.3
  54.7 0.7 copy.17
  55.3 0.5 copy.19
  55.9 0.0 copy-done.6
  55.9 1.5 maximum_bitcast_fusion
  57.4 5.8 %all-to-all-start = ((bf16[16,2,128,256]{3,2,1,0:T(8,128)(2,1)}), bf16[16,2,128,256]{3,2,1,0:T(8,128)(2,1)S(1)}, u32[]{:S(2)}, u32[]{:S(2)}) async-start(bf16[16,2,128,256]{3,2,1,0:T(8,128)(2,1)} %maximum_bitcast_fusion), calls=%async_computation | async-start | bytes 4194304 | tf_op jit(solution)/shard_map/all_to_all | solution.py:612
  63.2 0.0 copy-done.12
  63.2 0.6 fusion.27
  63.8 2.0 pad_add_fusion.tq_ref
  65.8 0.6 select_reduce_fusion.inv_ref
  66.4 43.1 %attention.3 = (bf16[128,2048]{1,0:T(8,128)(2,1)}, bf16[128,2048]{1,0:T(8,128)(2,1)}, bf16[128,2048]{1,0:T(8,128)(2,1)}, bf16[128,2048]{1,0:T(8,128)(2,1)}, bf16[2048,512]{1,0:T(8,128)(2,1)}) custom-call(s32[3]{0:T(128)} %pad_add_fusion.tq_ref, s32[16]{0:T(128)} %select_reduce_fusion.inv_ref, bf16[128,4096]{1,0:T(8,128)(2,1)} %get-tuple-element.56.act_u.q_own, ...), custom_call_target="tpu_custom_call" | custom-call | flops 15032385536 | bytes 16777216 | tf_op jit(solution)/shard_map/attention/pallas_call | solution.py:120
  109.5 0.0 all-to-all-done.act_hbm
  109.5 0.0 copy-start.5
  109.5 1.4 copy-done.5
  110.9 4.4 %all-to-all-start.1 = ((bf16[8,256,512]{2,1,0:T(8,128)(2,1)}), bf16[8,256,512]{2,1,0:T(8,128)(2,1)}, u32[]{:S(2)}, u32[]{:S(2)}) async-start(bf16[8,256,512]{2,1,0:T(8,128)(2,1)} %bitcast.61), calls=%async_computation.1 | async-start | bytes 4194304 | tf_op jit(solution)/shard_map/all_to_all | solution.py:616
  115.3 0.0 copy-start.15
  115.3 0.0 copy-start.14
  115.3 57.8 %attention.2 = (bf16[128,2048]{1,0:T(8,128)(2,1)}, bf16[128,2048]{1,0:T(8,128)(2,1)}, bf16[128,2048]{1,0:T(8,128)(2,1)}, bf16[128,2048]{1,0:T(8,128)(2,1)}, bf16[2048,512]{1,0:T(8,128)(2,1)}) custom-call(s32[3]{0:T(128)} %pad_add_fusion.tq_ref, s32[16]{0:T(128)} %select_reduce_fusion.inv_ref, bf16[128,4096]{1,0:T(8,128)(2,1)} %get-tuple-element.55.act_d.q_own, ...), custom_call_target="tpu_custom_call" | custom-call | flops 15032385536 | bytes 16777216 | tf_op jit(solution)/shard_map/attention/pallas_call | solution.py:120
  173.1 1.4 collective-permute-start
  174.4 1.6 collective-permute-start.1
  176.0 0.0 copy-done.15
  176.0 3.8 %collective-permute-start.2 = (bf16[128,2048]{1,0:T(8,128)(2,1)S(1)}, bf16[128,2048]{1,0:T(8,128)(2,1)S(1)}, u32[]{:S(2)}, u32[]{:S(2)}) collective-permute-start(bf16[128,2048]{1,0:T(8,128)(2,1)S(1)} %copy-done.15), channel_id=1, source_target_pairs={{0,112},{1,113},{2,114},{3,115},{4,116},{5,117},{6,118},{7,119},{8... | collective-permute-start | bytes 1572872 | tf_op jit(solution)/shard_map/ppermute | solution.py:592
  179.8 0.0 copy-done.14
  179.8 0.4 collective-permute-start.3
  180.2 0.0 all-to-all-done.1.parts_u
  180.3 81.4 %finish.1 = (bf16[128,4096]{1,0:T(8,128)(2,1)}, bf16[128,4096]{1,0:T(8,128)(2,1)}, f32[256,1024]{1,0:T(8,128)}, f32[1,256]{1,0:T(1,128)}) custom-call(bf16[2048,512]{1,0:T(8,128)(2,1)} %get-tuple-element.54.terms_d, bf16[8,256,512]{2,1,0:T(8,128)(2,1)} %all-to-all-done.1.parts_u, bf16[128,2048]{1,0:T(8,128)(2,1)} %get-tuple-element.59.dqo_d, ...), custom_call_target="tpu_custom_call" | custom-call | tf_op jit(solution)/shard_map/finish/pallas_call | solution.py:558
  261.6 0.0 collective-permute-done
  261.7 0.0 collective-permute-done.1
  261.7 0.0 collective-permute-done.2
  261.7 0.0 collective-permute-done.3
  261.7 0.1 maximum_bitcast_fusion.1
  261.8 0.0 copy-start.11
  261.8 0.1 maximum_bitcast_fusion.2
  262.0 0.0 copy-start.10
  262.0 0.1 bitcast_dynamic-update-slice_fusion.1
  262.0 0.0 copy-start.8
  262.0 0.1 bitcast_dynamic-update-slice_fusion
  262.1 1.2 copy-done.11
  263.3 1.0 copy.27
  264.2 0.0 copy-done.10
  264.2 1.0 copy.28
  265.2 0.0 copy-done.7
  265.2 0.1 copy-done.9
  265.3 1.0 copy.29
  266.3 0.0 copy-done.13
  266.3 0.6 copy.30
  (9 shorter events, 0.0 us)
Async XLA Ops:
  0.6 3.9 %copy-start = (bf16[1,128,4096]{2,1,0:T(8,128)(2,1)S(1)}, bf16[1,128,4096]{2,1,0:T(8,128)(2,1)}, u32[]{:S(2)}) copy-start(bf16[1,128,4096]{2,1,0:T(8,128)(2,1)} %param.7) | copy-start | bytes 3145732
  4.6 5.6 %copy-start.1 = (bf16[1,128,4096]{2,1,0:T(8,128)(2,1)S(1)}, bf16[1,128,4096]{2,1,0:T(8,128)(2,1)}, u32[]{:S(2)}) copy-start(bf16[1,128,4096]{2,1,0:T(8,128)(2,1)} %param.8) | copy-start | bytes 3145732
  4.6 9.3 %copy-start.2 = (bf16[2,1,4096,1024]{3,2,1,0:T(8,128)(2,1)S(1)}, bf16[2,1,4096,1024]{3,2,1,0:T(8,128)(2,1)}, u32[]{:S(2)}) copy-start(bf16[2,1,4096,1024]{3,2,1,0:T(8,128)(2,1)} %weights.1) | copy-start | bytes 50331652
  16.6 36.0 %copy-start.4 = (bf16[128,4096]{1,0:T(8,128)(2,1)S(1)}, bf16[128,4096]{1,0:T(8,128)(2,1)}, u32[]{:S(2)}) copy-start(bf16[128,4096]{1,0:T(8,128)(2,1)} %get-tuple-element.56.act_u.q_own) | copy-start | bytes 3145732
  52.7 2.0 copy-start.3
  54.7 1.2 copy-start.6
  57.4 5.8 %copy-start.12 = (s32[16]{0:T(128)S(1)}, s32[16]{0:T(128)}, u32[]{:S(2)}) copy-start(s32[16]{0:T(128)} %param.13) | copy-start | bytes 196
  57.4 52.1 %all-to-all-start = ((bf16[16,2,128,256]{3,2,1,0:T(8,128)(2,1)}), bf16[16,2,128,256]{3,2,1,0:T(8,128)(2,1)S(1)}, u32[]{:S(2)}, u32[]{:S(2)}) async-start(bf16[16,2,128,256]{3,2,1,0:T(8,128)(2,1)} %maximum_bitcast_fusion), calls=%async_computation | async-start | bytes 4194304 | tf_op jit(solution)/shard_map/all_to_all | solution.py:612
  109.5 1.4 copy-start.5
  110.9 69.3 %all-to-all-start.1 = ((bf16[8,256,512]{2,1,0:T(8,128)(2,1)}), bf16[8,256,512]{2,1,0:T(8,128)(2,1)}, u32[]{:S(2)}, u32[]{:S(2)}) async-start(bf16[8,256,512]{2,1,0:T(8,128)(2,1)} %bitcast.61), calls=%async_computation.1 | async-start | bytes 4194304 | tf_op jit(solution)/shard_map/all_to_all | solution.py:616
  115.3 60.8 %copy-start.15 = (bf16[128,2048]{1,0:T(8,128)(2,1)S(1)}, bf16[128,2048]{1,0:T(8,128)(2,1)}, u32[]{:S(2)}) copy-start(bf16[128,2048]{1,0:T(8,128)(2,1)} %get-tuple-element.52) | copy-start | bytes 1572868
  115.3 64.6 %copy-start.14 = (bf16[128,2048]{1,0:T(8,128)(2,1)S(1)}, bf16[128,2048]{1,0:T(8,128)(2,1)}, u32[]{:S(2)}) copy-start(bf16[128,2048]{1,0:T(8,128)(2,1)} %get-tuple-element.53) | copy-start | bytes 1572868
  173.1 88.6 %collective-permute-start = (bf16[128,2048]{1,0:T(8,128)(2,1)}, bf16[128,2048]{1,0:T(8,128)(2,1)S(1)}, u32[]{:S(2)}, u32[]{:S(2)}) collective-permute-start(bf16[128,2048]{1,0:T(8,128)(2,1)} %get-tuple-element.46), channel_id=1, source_target_pairs={{0,16},{1,17},{2,18},{3,19},{4,20},{5,21},{6,22},{7,23},{8,24},{9,... | collective-permute-start | bytes 1572872 | tf_op jit(solution)/shard_map/ppermute | solution.py:592
  174.4 87.2 %collective-permute-start.1 = (bf16[128,2048]{1,0:T(8,128)(2,1)}, bf16[128,2048]{1,0:T(8,128)(2,1)S(1)}, u32[]{:S(2)}, u32[]{:S(2)}) collective-permute-start(bf16[128,2048]{1,0:T(8,128)(2,1)} %get-tuple-element.47), channel_id=1, source_target_pairs={{0,17},{1,16},{2,19},{3,18},{4,21},{5,20},{6,23},{7,22},{8,25},{9,... | collective-permute-start | bytes 1572872 | tf_op jit(solution)/shard_map/ppermute | solution.py:593
  176.0 85.6 %collective-permute-start.2 = (bf16[128,2048]{1,0:T(8,128)(2,1)S(1)}, bf16[128,2048]{1,0:T(8,128)(2,1)S(1)}, u32[]{:S(2)}, u32[]{:S(2)}) collective-permute-start(bf16[128,2048]{1,0:T(8,128)(2,1)S(1)} %copy-done.15), channel_id=1, source_target_pairs={{0,112},{1,113},{2,114},{3,115},{4,116},{5,117},{6,118},{7,119},{8... | collective-permute-start | bytes 1572872 | tf_op jit(solution)/shard_map/ppermute | solution.py:592
  179.8 81.8 %collective-permute-start.3 = (bf16[128,2048]{1,0:T(8,128)(2,1)S(1)}, bf16[128,2048]{1,0:T(8,128)(2,1)S(1)}, u32[]{:S(2)}, u32[]{:S(2)}) collective-permute-start(bf16[128,2048]{1,0:T(8,128)(2,1)S(1)} %copy-done.14), channel_id=1, source_target_pairs={{0,113},{1,112},{2,115},{3,114},{4,117},{5,116},{6,119},{7,118},{8... | collective-permute-start | bytes 1572872 | tf_op jit(solution)/shard_map/ppermute | solution.py:593
  261.8 1.4 copy-start.11
  262.0 2.3 copy-start.10
  262.0 3.2 %copy-start.8 = (bf16[1,128,4096]{2,1,0:T(8,128)(2,1)}, bf16[1,128,4096]{2,1,0:T(8,128)(2,1)S(1)}, u32[]{:S(2)}) copy-start(bf16[1,128,4096]{2,1,0:T(8,128)(2,1)S(1)} %bitcast_dynamic-update-slice_fusion.1) | copy-start | bytes 3145732
  263.3 2.0 copy-start.7
  263.3 2.1 copy-start.9
  264.2 2.1 copy-start.13
